TPU v7x, 32 devices: a whole 2x2x4 slice. The times are simulated.
32 devices in a mesh: tm: 4 (over x, core), site: 8 (over z, y).
Axes of the slice: x: 2, y: 2, z: 4, core: 2. Of those that a mesh axis runs over, the one named last changes fastest.
Arguments:
- source: float32 [16, 8, 6144], P('tm', None, 'site')
- aux_field: float32 [16, 6144], P('tm', 'site'), may hold values from -2 to 2
- hopping_exp: float32 [6144, 6144], P('site'), as said below
Outputs:
- solution_field: float32 [16, 8, 6144], P('tm', None, 'site')
- residual: float32 [16, 8, 6144], P('tm', None, 'site')
Inputs may be any that keep to these rules, and one draw needn't show every extreme that they name: hopping_exp is exactly symmetric and positive definite.
All inputs are finite; a program needn't handle non-finite values.
Results may differ from a plain program's by a relative error of at most 0.00024.
Values sent between devices are 32-bit elements; how exact they have to be, the bound alone decides.
A program may use at most 64 MiB of HBM per device.

v0:
```python
import jax
import jax.numpy as jnp
from jax import lax
from jax.sharding import PartitionSpec as P

ITERS = 2


def passed_along(block, axis, distance):
    devices = range(lax.axis_size(axis))
    route = [((i - distance) % len(devices), i) for i in devices]
    return lax.ppermute(block, axis, route)


def kernel_fold(column_major, piece):
    return jnp.einsum("trc,cs->trs", piece, column_major, precision=lax.Precision.HIGHEST)


def forward_kernel(field, column_major):
    return kernel_fold(column_major, lax.all_gather(field, "site", axis=2, tiled=True))


def adjoint_kernel(field, column_major):
    return kernel_fold(column_major, lax.all_gather(field, "site", axis=2, tiled=True))


def forward_apply(field, boost, column_major):
    tm_index = lax.axis_index("tm")
    image = forward_kernel(field, column_major)
    prior = passed_along(image[-1], "tm", 1)
    prior = jnp.where(tm_index == 0, -prior, prior)
    shifted = jnp.concatenate([prior[None], image[:-1]], axis=0)
    return field - boost[:, None, :] * shifted


def adjoint_apply(field, boost, column_major):
    tm_index = lax.axis_index("tm")
    last_index = lax.axis_size("tm") - 1
    boosted = boost[:, None, :] * field
    image = adjoint_kernel(boosted, column_major)
    following = passed_along(image[0], "tm", -1)
    following = jnp.where(tm_index == last_index, -following, following)
    shifted = jnp.concatenate([image[1:], following[None]], axis=0)
    return field - shifted


def on_device(source, aux_field, hopping_exp):
    column_major = jnp.transpose(hopping_exp)
    boost = jnp.exp(aux_field)
    solution_field = jnp.zeros_like(source)
    residual = source
    direction = source
    norm_now = lax.psum(jnp.sum(residual * residual, axis=(0, 2)), ("tm", "site"))
    for iteration in range(ITERS):
        forward = forward_apply(direction, boost, column_major)
        image = adjoint_apply(forward, boost, column_major)
        curvature = lax.psum(jnp.sum(direction * image, axis=(0, 2)), ("tm", "site"))
        alpha = (norm_now / curvature)[None, :, None]
        solution_field = solution_field + alpha * direction
        residual = residual - alpha * image
        if iteration + 1 < ITERS:
            norm_next = lax.psum(jnp.sum(residual * residual, axis=(0, 2)), ("tm", "site"))
            direction = residual + (norm_next / norm_now)[None, :, None] * direction
            norm_now = norm_next
    return (solution_field, residual)


def solution(mesh):
    placed = (P("tm", None, "site"), P("tm", "site"), P("site", None))
    return jax.shard_map(
        on_device,
        mesh=mesh,
        in_specs=placed,
        out_specs=(P("tm", None, "site"), P("tm", None, "site")),
        check_vma=False,
    )
```

profile of v0, /device:TPU:0, one launch (start us, length us, event | category | flops | bytes accessed | tf_op | source)
XLA Modules:
  0.0 338.4 jit_solution(7928377051968209476)
XLA Ops:
  0.6 0.0 copy-start
  0.6 0.0 copy-start.1
  0.6 34.1 %all_gather.12 = f32[4,8,6144]{2,1,0:T(8,128)S(1)} all-gather(f32[4,8,768]{2,1,0:T(8,128)} %param.3), channel_id=1, replica_groups=mesh['tm'=4,'site'=8] {'site'}, dimensions={2}, use_global_device_ids=true | all-gather | bytes 884736 | tf_op jit(solution)/shard_map/all_gather | solution.py:20
  34.8 19.5 %fusion.6 = f32[4,8,768]{2,1,0:T(8,128)S(1)} fusion(f32[4,8,6144]{2,1,0:T(8,128)S(1)} %all_gather.12, f32[768,6144]{1,0:T(8,128)} %param.5), kind=kOutput, calls=%fused_computation.6 | convolution fusion | flops 1811939328 | bytes 19759104 | tf_op jit(solution)/shard_map/trc,cs->trs/dot_general | solution.py:16
  54.3 0.1 collective-permute-start
  54.3 0.0 copy-done.1
  54.4 3.2 collective-permute-done
  57.6 0.0 copy-done
  57.6 32.2 %all_gather.13 = f32[4,8,6144]{2,1,0:T(8,128)S(1)} all-gather(f32[4,8,768]{2,1,0:T(8,128)S(1)} %broadcast_multiply_fusion.1), channel_id=1, replica_groups=mesh['tm'=4,'site'=8] {'site'}, dimensions={2}, use_global_device_ids=true | all-gather | bytes 884736 | tf_op jit(solution)/shard_map/all_gather | solution.py:24
  89.8 19.5 %fusion.4 = f32[4,8,768]{2,1,0:T(8,128)S(1)} fusion(f32[4,8,6144]{2,1,0:T(8,128)S(1)} %all_gather.13, f32[768,6144]{1,0:T(8,128)} %param.5), kind=kOutput, calls=%fused_computation.4 | convolution fusion | flops 1811939328 | bytes 19759104 | tf_op jit(solution)/shard_map/trc,cs->trs/dot_general | solution.py:16
  109.3 0.0 slice-start
  109.4 0.1 collective-permute-start.1
  109.4 1.5 collective-permute-done.1
  110.9 0.2 multiply_reduce_fusion.2
  111.1 39.9 %all-reduce = (f32[8]{0:T(128)S(1)}, f32[8]{0:T(128)S(1)}) all-reduce(f32[8]{0:T(128)S(1)} %get-tuple-element.3, f32[8]{0:T(128)S(1)} %get-tuple-element.2), channel_id=1, replica_groups=mesh['tm'=4,'site'=8] {'tm','site'}, use_global_device_ids=true, to_apply=%region_1.0 | all-reduce | flops 16 | bytes 128 | tf_op jit(solution)/shard_map/psum | solution.py:53
  151.0 0.2 multiply_reduce_fusion.1
  151.2 40.4 %psum.30 = f32[8]{0:T(128)S(1)} all-reduce(f32[8]{0:T(128)S(1)} %get-tuple-element.6), channel_id=1, replica_groups=mesh['tm'=4,'site'=8] {'tm','site'}, use_global_device_ids=true, to_apply=%region_5.6 | all-reduce | flops 8 | bytes 64 | tf_op jit(solution)/shard_map/psum | solution.py:62
  191.6 0.1 multiply_add_fusion.1
  191.7 32.3 %all_gather.14 = f32[4,8,6144]{2,1,0:T(8,128)S(1)} all-gather(f32[4,8,768]{2,1,0:T(8,128)S(1)} %multiply_add_fusion.1), channel_id=1, replica_groups=mesh['tm'=4,'site'=8] {'site'}, dimensions={2}, use_global_device_ids=true | all-gather | bytes 884736 | tf_op jit(solution)/shard_map/all_gather | solution.py:20
  223.9 0.0 slice-start.1
  223.9 0.0 slice-start.2
  223.9 0.0 slice-start.3
  223.9 0.0 slice-start.4
  224.0 19.6 %fusion.2 = f32[4,8,768]{2,1,0:T(8,128)S(1)} fusion(f32[4,8,6144]{2,1,0:T(8,128)S(1)} %all_gather.14, f32[768,6144]{1,0:T(8,128)} %param.5), kind=kOutput, calls=%fused_computation.2 | convolution fusion | flops 1811939328 | bytes 19759104 | tf_op jit(solution)/shard_map/trc,cs->trs/dot_general | solution.py:16
  243.6 0.1 collective-permute-start.2
  243.7 3.2 collective-permute-done.2
  247.0 32.1 %all_gather.15 = f32[4,8,6144]{2,1,0:T(8,128)S(1)} all-gather(f32[4,8,768]{2,1,0:T(8,128)S(1)} %broadcast_multiply_fusion), channel_id=1, replica_groups=mesh['tm'=4,'site'=8] {'site'}, dimensions={2}, use_global_device_ids=true | all-gather | bytes 884736 | tf_op jit(solution)/shard_map/all_gather | solution.py:24
  279.0 0.0 slice-done
  279.0 0.0 slice-done.1
  279.0 0.0 slice-done.2
  279.0 0.0 slice-done.3
  279.0 0.0 slice-done.4
  279.1 16.8 %fusion = f32[4,8,768]{2,1,0:T(8,128)S(1)} fusion(f32[4,8,6144]{2,1,0:T(8,128)S(1)} %all_gather.15, f32[768,6144]{1,0:T(8,128)S(1)} %bitcast.30), kind=kOutput, calls=%fused_computation | convolution fusion | flops 1811939328 | bytes 19759104 | tf_op jit(solution)/shard_map/trc,cs->trs/dot_general | solution.py:16
  295.9 0.1 collective-permute-start.3
  296.0 1.5 collective-permute-done.3
  297.5 0.1 multiply_reduce_fusion
  297.6 39.9 %psum.31 = f32[8]{0:T(128)S(1)} all-reduce(f32[8]{0:T(128)S(1)} %multiply_reduce_fusion), channel_id=1, replica_groups=mesh['tm'=4,'site'=8] {'tm','site'}, use_global_device_ids=true, to_apply=%region_7.8 | all-reduce | flops 8 | bytes 64 | tf_op jit(solution)/shard_map/psum | solution.py:57
  337.6 0.8 multiply_subtract_fusion
  (19 shorter events, 0.1 us)
Async XLA Ops:
  0.6 56.9 %copy-start = (f32[4,8,768]{2,1,0:T(8,128)S(1)}, f32[4,8,768]{2,1,0:T(8,128)}, u32[]{:S(2)}) copy-start(f32[4,8,768]{2,1,0:T(8,128)} %param.3) | copy-start | bytes 294916
  0.6 53.7 %copy-start.1 = (f32[4,768]{1,0:T(4,128)S(1)}, f32[4,768]{1,0:T(4,128)}, u32[]{:S(2)}) copy-start(f32[4,768]{1,0:T(4,128)} %param.4) | copy-start | bytes 36868
  54.3 3.3 collective-permute-start
  109.3 169.7 %slice-start = ((s8[18874368]{0:T(1024)(128)(4,1)}), s8[2097152]{0:T(1024)(128)(4,1)S(1)}, s32[]{:S(2)}) async-start(s8[18874368]{0:T(1024)(128)(4,1)} %bitcast.29), calls=%async_computation | async-start | bytes 4194304
  109.4 1.6 collective-permute-start.1
  223.9 55.1 %slice-start.1 = ((s8[18874368]{0:T(1024)(128)(4,1)}), s8[4194304]{0:T(1024)(128)(4,1)S(1)}, s32[]{:S(2)}) async-start(s8[18874368]{0:T(1024)(128)(4,1)} %bitcast.29), calls=%async_computation.1 | async-start | bytes 8388608
  223.9 55.1 %slice-start.2 = ((s8[18874368]{0:T(1024)(128)(4,1)}), s8[4194304]{0:T(1024)(128)(4,1)S(1)}, s32[]{:S(2)}) async-start(s8[18874368]{0:T(1024)(128)(4,1)} %bitcast.29), calls=%async_computation.2 | async-start | bytes 8388608
  223.9 55.1 %slice-start.3 = ((s8[18874368]{0:T(1024)(128)(4,1)}), s8[4194304]{0:T(1024)(128)(4,1)S(1)}, s32[]{:S(2)}) async-start(s8[18874368]{0:T(1024)(128)(4,1)} %bitcast.29), calls=%async_computation.3 | async-start | bytes 8388608
  223.9 55.1 %slice-start.4 = ((s8[18874368]{0:T(1024)(128)(4,1)}), s8[4194304]{0:T(1024)(128)(4,1)S(1)}, s32[]{:S(2)}) async-start(s8[18874368]{0:T(1024)(128)(4,1)} %bitcast.29), calls=%async_computation.4 | async-start | bytes 8388608
  243.6 3.3 collective-permute-start.2
  295.9 1.6 collective-permute-start.3
where the time goes:
time: 339 us; the launch traced here: 338 us
  blocking collectives  251 us (74%)
  matrix products  75.5 us (22%)
  waiting for transfers between devices  9.4 us (3%)
    psum x2, blocking collectives, on_device(): lax.psum(jnp.sum(residual * residual, axis=(0, 2)), ('tm', 'site'))  80.3 us
    dot_general x4, matrix products, kernel_fold(): jnp.einsum('trc,cs->trs', piece, column_major, precision=lax.Precision.HI...  75.5 us
    all_gather x2, blocking collectives, forward_kernel(): lax.all_gather(field, 'site', axis=2, tiled=True)  66.4 us
    all_gather x2, blocking collectives, adjoint_kernel(): lax.all_gather(field, 'site', axis=2, tiled=True)  64.3 us
    psum x1, blocking collectives, on_device(): lax.psum(jnp.sum(direction * image, axis=(0, 2)), ('tm', 'site'))  39.9 us
    ppermute x4, waiting for transfers between devices, passed_along(): return lax.ppermute(block, axis, route)  9.4 us
  transfers between devices with their start and end apart: 4, of which 4 were waited for; matrix products, arithmetic and copies ran while one was open for 0% of the time, Pallas kernels for 0%

commit v1 on v0

--- a/solution.py
+++ b/solution.py
@@ -1,6 +1,10 @@
+import functools
+
 import jax
 import jax.numpy as jnp
 from jax import lax
+from jax.experimental import pallas as pl
+from jax.experimental.pallas import tpu as pltpu
 from jax.sharding import PartitionSpec as P
 
 ITERS = 2
@@ -44,7 +48,7 @@
     return field - shifted
 
 
-def on_device(source, aux_field, hopping_exp):
+def plain_solve(source, aux_field, hopping_exp):
     column_major = jnp.transpose(hopping_exp)
     boost = jnp.exp(aux_field)
     solution_field = jnp.zeros_like(source)
@@ -65,6 +69,246 @@
     return (solution_field, residual)
 
 
+MESH = pl.DeviceIdType.MESH
+TRANSPOSED = (((1,), (1,)), ((), ()))
+LANES = 128
+APPLIES = 2 * ITERS
+SUMS = 3
+STAGES = 4
+
+
+def crossed(index, mask):
+    bit = 1
+    while bit <= mask:
+        if mask & bit:
+            index = index + bit - 2 * bit * ((index // bit) % 2)
+        bit *= 2
+    return index
+
+
+def lane_sums(block):
+    folded = jnp.sum(block * block, axis=0)
+    total = folded[:, :LANES]
+    for start in range(LANES, folded.shape[1], LANES):
+        total = total + folded[:, start : start + LANES]
+    return total
+
+
+def solve_kernel(
+    tm_size, n, source, aux, hopping, solution_out, residual_out,
+    high, low, stage, held, edge, boost, image_first, residual, direction, tm_sums, site_sums,
+    stage_sem, own_send, pass_send, edge_send, recv, tm_send, tm_recv, site_send, site_recv,
+):
+    slices, rhs, width = source.shape
+    tm, site = lax.axis_index("tm"), lax.axis_index("site")
+    unwaited = []
+
+    def load(slot):
+        first = pl.multiple_of(crossed(site, slot) * width, width)
+        return pltpu.make_async_copy(hopping.at[:, pl.ds(first, width)], stage.at[slot % STAGES], stage_sem.at[slot])
+
+    for slot in range(min(STAGES, n)):
+        load(slot).start()
+
+    barrier = pltpu.get_barrier_semaphore()
+    for mask in range(1, tm_size):
+        pl.semaphore_signal(barrier, inc=1, device_id=(crossed(tm, mask), site), device_id_type=MESH)
+    for mask in range(1, n):
+        pl.semaphore_signal(barrier, inc=1, device_id=(tm, crossed(site, mask)), device_id_type=MESH)
+
+    for t in range(slices):
+        boost[t] = jnp.broadcast_to(jnp.exp(aux[t : t + 1, :]), (rhs, width))
+
+    pl.semaphore_wait(barrier, tm_size - 1 + n - 1)
+
+    def send(src, dst, send_sem, recv_sem, device):
+        copy = pltpu.make_async_remote_copy(
+            src_ref=src, dst_ref=dst, send_sem=send_sem, recv_sem=recv_sem, device_id=device, device_id_type=MESH
+        )
+        copy.start()
+        unwaited.append(copy)
+
+    def arrived(ref, sem):
+        pltpu.make_async_copy(ref, ref, sem).wait()
+
+    def sum_rows(which):
+        return pl.ds(0, 2 * rhs if which == 0 else rhs)
+
+    def sum_over_tm(which):
+        rows = sum_rows(which)
+        for mask in range(1, tm_size):
+            send(tm_sums.at[which, 0, rows], tm_sums.at[which, mask, rows], tm_send.at[which, mask],
+                 tm_recv.at[which, mask], (crossed(tm, mask), site))
+
+    def sum_over_site(which):
+        rows = sum_rows(which)
+        total = tm_sums[which, 0, rows]
+        for mask in range(1, tm_size):
+            arrived(tm_sums.at[which, mask, rows], tm_recv.at[which, mask])
+            total = total + tm_sums[which, mask, rows]
+        site_sums[which, 0, rows] = total
+        for mask in range(1, n):
+            send(site_sums.at[which, 0, rows], site_sums.at[which, mask, rows], site_send.at[which, mask],
+                 site_recv.at[which, mask], (tm, crossed(site, mask)))
+
+    def summed(which):
+        rows = sum_rows(which)
+        total = site_sums[which, 0, rows]
+        for mask in range(1, n):
+            arrived(site_sums.at[which, mask, rows], site_recv.at[which, mask])
+            total = total + site_sums[which, mask, rows]
+        return jnp.sum(total, axis=1, keepdims=True)
+
+    def split(slot):
+        load(slot).wait()
+        step = width // 8
+
+        @pl.loop(0, width, step=step)
+        def _(row):
+            rows = pl.ds(pl.multiple_of(row, step), step)
+            value = stage[slot % STAGES, rows, :]
+            upper = value.astype(jnp.bfloat16)
+            high[slot, rows, :] = upper
+            low[slot, rows, :] = (value - upper.astype(jnp.float32)).astype(jnp.bfloat16)
+
+        if slot + STAGES < n:
+            load(slot + STAGES).start()
+
+    def product(turn, slot):
+        value = held[turn, slot].reshape(slices * rhs, width)
+        upper = value.astype(jnp.bfloat16)
+        lower = (value - upper.astype(jnp.float32)).astype(jnp.bfloat16)
+        both = lax.dot_general(
+            jnp.concatenate([upper, lower], axis=0), high[slot], TRANSPOSED, preferred_element_type=jnp.float32
+        )
+        rest = lax.dot_general(upper, low[slot], TRANSPOSED, preferred_element_type=jnp.float32)
+        return both[: slices * rhs] + (both[slices * rhs :] + rest)
+
+    def apply(turn, field, pending):
+        forward = turn % 2 == 0
+        own = pl.ds(1 if forward else 0, slices - 1)
+        far = pl.ds(0 if forward else slices - 1, 1)
+        if forward:
+            edge[turn] = field[slices - 1 :]
+            held[turn, 0, own] = field[: slices - 1]
+            target = lax.rem(tm + 1, tm_size)
+        else:
+            edge[turn] = field[:1]
+            held[turn, 0, own] = field[1:]
+            target = lax.rem(tm + tm_size - 1, tm_size)
+        send(edge.at[turn], held.at[turn, 0, far], edge_send.at[turn], recv.at[turn, 1, 0], (target, site))
+        near = [1] + list(range(2, n, 2))
+
+        def spread(part, which):
+            for slot in near:
+                send(held.at[turn, 0, part], held.at[turn, slot, part], own_send.at[turn, which, slot],
+                     recv.at[turn, which, slot], (tm, crossed(site, slot)))
+
+        spread(own, 0)
+        if pending is not None:
+            sum_over_tm(pending)
+        if turn == 0:
+            split(0)
+        arrived(held.at[turn, 0, far], recv.at[turn, 1, 0])
+        spread(far, 1)
+        total = product(turn, 0)
+        for position, slot in enumerate(near + list(range(3, n, 2))):
+            if turn == 0:
+                split(slot)
+            for which, part in ((0, own), (1, far)):
+                arrived(held.at[turn, slot, part], recv.at[turn, which, slot])
+                if slot % 2 == 0:
+                    send(held.at[turn, slot, part], held.at[turn, slot + 1, part], pass_send.at[turn, which, slot],
+                         recv.at[turn, which, slot + 1], (tm, crossed(site, 1)))
+            if position == 1 and pending is not None:
+                sum_over_site(pending)
+            total = total + product(turn, slot)
+        shifted = total.reshape(slices, rhs, width)
+        sign = jnp.where(tm == (0 if forward else tm_size - 1), -1.0, 1.0).astype(jnp.float32)
+        if forward:
+            return jnp.concatenate([sign * shifted[:1], shifted[1:]], axis=0)
+        return jnp.concatenate([shifted[: slices - 1], sign * shifted[slices - 1 :]], axis=0)
+
+    first = source[...] - boost[...] * apply(0, source[...], None)
+    image_first[...] = first
+    tm_sums[0, 0, pl.ds(0, rhs)] = lane_sums(source[...])
+    tm_sums[0, 0, pl.ds(rhs, rhs)] = lane_sums(first)
+
+    image = image_first[...] - apply(1, boost[...] * first, 0)
+    sums = summed(0)
+    norm_now, curvature = sums[:rhs], sums[rhs:]
+    alpha = norm_now / curvature
+    solution_out[...] = alpha * source[...]
+    after = source[...] - alpha * image
+    residual[...] = after
+    tm_sums[1, 0, pl.ds(0, rhs)] = lane_sums(after)
+
+    second = residual[...] - boost[...] * apply(2, after, 1)
+    norm_next = summed(1)
+    beta = norm_next / norm_now
+    direction[...] = residual[...] + beta * source[...]
+    second = second + beta * image_first[...]
+    image_first[...] = second
+    tm_sums[2, 0, pl.ds(0, rhs)] = lane_sums(second)
+
+    image = image_first[...] - apply(3, boost[...] * second, 2)
+    alpha = norm_next / summed(2)
+    solution_out[...] = solution_out[...] + alpha * direction[...]
+    residual_out[...] = residual[...] - alpha * image
+
+    for copy in unwaited:
+        copy.wait_send()
+
+
+def on_device(source, aux_field, hopping_exp):
+    tm_size, n = lax.axis_size("tm"), lax.axis_size("site")
+    slices, rhs, width = source.shape
+    fits = width % LANES == 0 and n >= 2 and n & (n - 1) == 0 and tm_size >= 2 and tm_size & (tm_size - 1) == 0
+    if not fits or slices < 2 or rhs % 8 or ITERS != 2:
+        return plain_solve(source, aux_field, hopping_exp)
+    field = jax.ShapeDtypeStruct(source.shape, jnp.float32)
+    local = pltpu.VMEM(source.shape, jnp.float32)
+    dma = pltpu.SemaphoreType.DMA
+    whole = pl.BlockSpec(memory_space=pltpu.VMEM)
+    return pl.pallas_call(
+        functools.partial(solve_kernel, tm_size, n),
+        out_shape=(field, field),
+        in_specs=[whole, whole, pl.BlockSpec(memory_space=pl.ANY)],
+        out_specs=(whole, whole),
+        scratch_shapes=[
+            pltpu.VMEM((n, width, width), jnp.bfloat16),
+            pltpu.VMEM((n, width, width), jnp.bfloat16),
+            pltpu.VMEM((STAGES, width, width), jnp.float32),
+            pltpu.VMEM((APPLIES, n, slices, rhs, width), jnp.float32),
+            pltpu.VMEM((APPLIES, 1, rhs, width), jnp.float32),
+            local,
+            local,
+            local,
+            local,
+            pltpu.VMEM((SUMS, tm_size, 2 * rhs, LANES), jnp.float32),
+            pltpu.VMEM((SUMS, n, 2 * rhs, LANES), jnp.float32),
+            dma((n,)),
+            dma((APPLIES, 2, n)),
+            dma((APPLIES, 2, n)),
+            dma((APPLIES,)),
+            dma((APPLIES, 2, n)),
+            dma((SUMS, tm_size)),
+            dma((SUMS, tm_size)),
+            dma((SUMS, n)),
+            dma((SUMS, n)),
+        ],
+        compiler_params=pltpu.CompilerParams(
+            collective_id=0, has_side_effects=True, vmem_limit_bytes=52 * 1024 * 1024
+        ),
+        cost_estimate=pl.CostEstimate(
+            flops=APPLIES * 6 * slices * rhs * n * width * width,
+            bytes_accessed=4 * n * width * width,
+            transcendentals=slices * width,
+        ),
+        name="conjugate_gradient",
+    )(source, aux_field, hopping_exp)
+
+
 def solution(mesh):
     placed = (P("tm", None, "site"), P("tm", "site"), P("site", None))
     return jax.shard_map(

time: 339 us -> 78.4 us (0.23)
  blocking collectives: 251 us -> 0 us
  matrix products: 75.5 us -> 0 us
  Pallas kernels: 0 us -> 74.7 us
  waiting for transfers between devices: 9.4 us -> 0 us
    all_gather x4 -> x0, blocking collectives: 131 us -> none  [the longest x2 66.4 us: forward_kernel(): lax.all_gather(field, 'site', axis=2, tiled=True)]
    psum x3 -> x0, blocking collectives: 120 us -> none  [the longest x2 80.3 us: on_device(): lax.psum(jnp.sum(residual * residual, axis=(0, 2)), ('tm', 'site'))]
    dot_general x4 -> x0, matrix products: 75.5 us -> none  [kernel_fold(): jnp.einsum('trc,cs->trs', piece, column_major, precision=lax.Precision.HI...]
    pallas_call x0 -> x1, Pallas kernels: none -> 74.7 us  [on_device(): pl.pallas_call(functools.partial(solve_kernel, tm_size, n), out_shape=(fi...]
    ppermute x4 -> x0, waiting for transfers between devices: 9.4 us -> none  [passed_along(): return lax.ppermute(block, axis, route)]
  transfers between devices with their start and end apart: 4 -> 0, of which waited for: 4 -> 0; matrix products, arithmetic and copies ran while one was open for 0% -> 0% of each run, Pallas kernels for 0% -> 0%
where the time goes in v1:
time: 78.4 us; the launch traced here: 78.2 us
  Pallas kernels  74.7 us (95%)
  local copies, waits for them, and re-layouts  2.88 us (4%)
    pallas_call x1, Pallas kernels, on_device(): pl.pallas_call(functools.partial(solve_kernel, tm_size, n), out_shape=(fi...  74.7 us
    unnamed x6, local copies, waits for them, and re-layouts  2.88 us

profile of v1, /device:TPU:0, one launch (start us, length us, event | category | flops | bytes accessed | tf_op | source)
XLA Modules:
  0.0 78.2 jit_solution(5211070567183302211)
XLA Ops:
  0.6 0.0 copy-start
  0.6 0.9 %copy-done = f32[4,8,768]{2,1,0:T(8,128)S(1)} copy-done((f32[4,8,768]{2,1,0:T(8,128)S(1)}, f32[4,8,768]{2,1,0:T(8,128)}, u32[]{:S(2)}) %copy-start) | copy-done | bytes 98328
  1.5 0.0 copy-start.1
  1.5 0.7 copy-done.1
  2.2 74.7 %conjugate_gradient.1 = (f32[4,8,768]{2,1,0:T(8,128)S(1)}, f32[4,8,768]{2,1,0:T(8,128)S(1)}) custom-call(f32[4,8,768]{2,1,0:T(8,128)S(1)} %copy-done, f32[4,768]{1,0:T(4,128)S(1)} %copy-done.1, f32[768,6144]{1,0:T(8,128)} %hopping.1), custom_call_target="tpu_custom_call" | custom-call | flops 3623878656 | bytes 18874368 | tf_op jit(solution)/shard_map/conjugate_gradient/pallas_call | solution.py:273
  76.9 0.6 copy.7
  77.5 0.6 copy.8
Async XLA Ops:
  0.6 0.9 %copy-start = (f32[4,8,768]{2,1,0:T(8,128)S(1)}, f32[4,8,768]{2,1,0:T(8,128)}, u32[]{:S(2)}) copy-start(f32[4,8,768]{2,1,0:T(8,128)} %source.1) | copy-start | bytes 294916
  1.5 0.7 copy-start.1

commit v2 on v1

--- a/solution.py
+++ b/solution.py
@@ -70,7 +70,7 @@
 
 
 MESH = pl.DeviceIdType.MESH
-TRANSPOSED = (((1,), (1,)), ((), ()))
+PLAIN = (((1,), (0,)), ((), ()))
 LANES = 128
 APPLIES = 2 * ITERS
 SUMS = 3
@@ -161,12 +161,12 @@
 
     def split(slot):
         load(slot).wait()
-        step = width // 8
+        step = LANES
 
         @pl.loop(0, width, step=step)
         def _(row):
             rows = pl.ds(pl.multiple_of(row, step), step)
-            value = stage[slot % STAGES, rows, :]
+            value = jnp.transpose(stage[slot % STAGES, :, rows])
             upper = value.astype(jnp.bfloat16)
             high[slot, rows, :] = upper
             low[slot, rows, :] = (value - upper.astype(jnp.float32)).astype(jnp.bfloat16)
@@ -179,9 +179,9 @@
         upper = value.astype(jnp.bfloat16)
         lower = (value - upper.astype(jnp.float32)).astype(jnp.bfloat16)
         both = lax.dot_general(
-            jnp.concatenate([upper, lower], axis=0), high[slot], TRANSPOSED, preferred_element_type=jnp.float32
+            jnp.concatenate([upper, lower], axis=0), high[slot], PLAIN, preferred_element_type=jnp.float32
         )
-        rest = lax.dot_general(upper, low[slot], TRANSPOSED, preferred_element_type=jnp.float32)
+        rest = lax.dot_general(upper, low[slot], PLAIN, preferred_element_type=jnp.float32)
         return both[: slices * rhs] + (both[slices * rhs :] + rest)
 
     def apply(turn, field, pending):

time: 78.4 us -> 74.3 us (0.948)
  Pallas kernels: 74.7 us -> 70.5 us
    pallas_call x1, Pallas kernels: 74.7 us -> 70.5 us  [on_device(): pl.pallas_call(functools.partial(solve_kernel, tm_size, n), out_shape=(fi...]
where the time goes in v2:
time: 74.3 us; the launch traced here: 74.1 us
  Pallas kernels  70.5 us (95%)
  local copies, waits for them, and re-layouts  2.88 us (4%)
    pallas_call x1, Pallas kernels, on_device(): pl.pallas_call(functools.partial(solve_kernel, tm_size, n), out_shape=(fi...  70.5 us
    unnamed x6, local copies, waits for them, and re-layouts  2.88 us

profile of v2, /device:TPU:0, one launch (start us, length us, event | category | flops | bytes accessed | tf_op | source)
XLA Modules:
  0.0 74.1 jit_solution(7069587861409771627)
XLA Ops:
  0.6 0.0 copy-start
  0.6 0.9 %copy-done = f32[4,8,768]{2,1,0:T(8,128)S(1)} copy-done((f32[4,8,768]{2,1,0:T(8,128)S(1)}, f32[4,8,768]{2,1,0:T(8,128)}, u32[]{:S(2)}) %copy-start) | copy-done | bytes 98328
  1.5 0.0 copy-start.1
  1.5 0.7 copy-done.1
  2.2 70.5 %conjugate_gradient.1 = (f32[4,8,768]{2,1,0:T(8,128)S(1)}, f32[4,8,768]{2,1,0:T(8,128)S(1)}) custom-call(f32[4,8,768]{2,1,0:T(8,128)S(1)} %copy-done, f32[4,768]{1,0:T(4,128)S(1)} %copy-done.1, f32[768,6144]{1,0:T(8,128)} %hopping.1), custom_call_target="tpu_custom_call" | custom-call | flops 3623878656 | bytes 18874368 | tf_op jit(solution)/shard_map/conjugate_gradient/pallas_call | solution.py:273
  72.8 0.6 copy.7
  73.4 0.6 copy.8
Async XLA Ops:
  0.6 0.9 %copy-start = (f32[4,8,768]{2,1,0:T(8,128)S(1)}, f32[4,8,768]{2,1,0:T(8,128)}, u32[]{:S(2)}) copy-start(f32[4,8,768]{2,1,0:T(8,128)} %source.1) | copy-start | bytes 294916
  1.5 0.7 copy-start.1
